TPU v7x, 128 devices: a whole 4x4x4 slice. The times are simulated.
128 devices in a mesh: seq: 32 (over z, y, core), head: 4 (over x).
Axes of the slice: x: 4, y: 4, z: 4, core: 2. Of those that a mesh axis runs over, the one named last changes fastest.
Arguments:
- query_states: bfloat16 [8192, 1536], P('seq', 'head'), may hold values from -100 to 100
- key_states: bfloat16 [8192, 1536], P('seq', 'head'), may hold values from -4.1 to 4.1
- value_states: bfloat16 [8192, 1536], P('seq', 'head'), may hold values from -6 to 6
- out_weight: bfloat16 [1536, 1536], P('head'), may hold values from -0.15625 to 0.15625
- out_grad: bfloat16 [8192, 1536], P(('seq', 'head')), may hold values from -6 to 6
- placement: int32 [32], replicated, may hold values from 0 to 31, each once
- sink_ids: int32 [256], replicated, may hold values from 0 to 8191, as said below
- span_mask: int32 [32, 32], replicated, may hold values from 0 to 1, as said below
Outputs:
- mixed: bfloat16 [8192, 1536], P(('seq', 'head'))
- query_grad: bfloat16 [8192, 1536], P('seq', 'head')
- key_grad: bfloat16 [8192, 1536], P('seq', 'head')
- value_grad: bfloat16 [8192, 1536], P('seq', 'head')
Inputs may be any that keep to these rules, and one draw needn't show every extreme that they name: `sink_ids`: 256 distinct row positions. The spans form contiguous runs of consecutive span numbers, starting with span 0; span_mask[c, e] is 1 when e lies in the run of c or in an earlier run, and 0 when e lies in a later run.
All inputs are finite; a program needn't handle non-finite values.
Results may differ from a plain program's by a relative error of at most 0.04.
Values may be sent and summed in bfloat16 or wider, within the bound.
A program may use at most 128 MiB of HBM per device.

v0:
```python
import jax
import jax.numpy as jnp
from jax import lax
from jax.sharding import PartitionSpec as P

HD = 128


def block_flags(count, rows, table):
    blocks = jnp.arange(count, dtype=jnp.int32) // rows
    hits = blocks[:, None] == jnp.arange(table.shape[0], dtype=jnp.int32)[None, :]
    return jnp.any(hits & (table[None, :] == 1), axis=1)


def sink_flags(count, sink_ids):
    positions = jnp.arange(count, dtype=jnp.int32)
    return jnp.any(positions[:, None] == sink_ids[None, :], axis=1)


def on_device(
    query_states, key_states, value_states, out_weight, out_grad, placement, sink_ids, span_mask
):
    rows = query_states.shape[0]
    heads = query_states.shape[1] // HD
    mine = lax.axis_index("seq")
    scale = HD ** (-0.5)
    my_span = placement[mine]
    row_allow = jnp.take(span_mask[my_span], placement)
    col_allow = jnp.take(span_mask[:, my_span], placement)
    queries = query_states.reshape(rows, heads, HD)
    own_keys = key_states.reshape(rows, heads, HD)
    own_values = value_states.reshape(rows, heads, HD)
    own_spots = mine * rows + jnp.arange(rows, dtype=jnp.int32)
    own_sink = jnp.any(own_spots[:, None] == sink_ids[None, :], axis=1)

    def key_mask(count):
        return block_flags(count, rows, row_allow) | sink_flags(count, sink_ids)

    key_part = lax.all_gather(key_states, "seq", axis=0, tiled=True)
    value_part = lax.all_gather(value_states, "seq", axis=0, tiled=True)
    count = key_part.shape[0]
    key_part = key_part.reshape(count, heads, HD)
    value_part = value_part.reshape(count, heads, HD)
    scores = (
        jnp.einsum("qhd,khd->qhk", queries, key_part, preferred_element_type=jnp.float32) * scale
    )
    scores = jnp.where(key_mask(count)[None, None, :], scores, -jnp.inf)
    top_old = jnp.full((rows, heads), -1e30, jnp.float32)
    top_new = jnp.maximum(top_old, jnp.max(scores, axis=-1))
    weights = jnp.exp(scores - top_new[..., None])
    total = jnp.sum(weights, axis=-1)
    summed = jnp.einsum(
        "qhk,khd->qhd", weights.astype(jnp.bfloat16), value_part, preferred_element_type=jnp.float32
    )
    forward = (top_new, total, summed)
    top, total, summed = forward
    attn = (summed / total[..., None]).astype(jnp.bfloat16).reshape(rows, -1)
    log_total = top + jnp.log(total)
    mixed = lax.psum_scatter(
        jnp.dot(attn, out_weight, preferred_element_type=jnp.float32).astype(jnp.bfloat16),
        "head",
        scatter_dimension=0,
        tiled=True,
    )
    d_attn = lax.dot_general(
        lax.all_gather(out_grad, "head", axis=0, tiled=True),
        out_weight,
        (((1,), (1,)), ((), ())),
        preferred_element_type=jnp.float32,
    ).astype(jnp.bfloat16)
    grad_heads = d_attn.reshape(rows, heads, HD)
    delta = jnp.sum(
        grad_heads.astype(jnp.float32) * attn.reshape(rows, heads, HD).astype(jnp.float32), axis=-1
    )
    key_part = lax.all_gather(key_states, "seq", axis=0, tiled=True)
    value_part = lax.all_gather(value_states, "seq", axis=0, tiled=True)
    count = key_part.shape[0]
    key_part = key_part.reshape(count, heads, HD)
    value_part = value_part.reshape(count, heads, HD)
    scores = (
        jnp.einsum("qhd,khd->qhk", queries, key_part, preferred_element_type=jnp.float32) * scale
    )
    probs = jnp.where(key_mask(count)[None, None, :], jnp.exp(scores - log_total[..., None]), 0.0)
    dots = jnp.einsum("qhd,khd->qhk", grad_heads, value_part, preferred_element_type=jnp.float32)
    grads = probs * (dots - delta[..., None])
    query_grad = (
        jnp.einsum(
            "qhk,khd->qhd", grads.astype(jnp.bfloat16), key_part, preferred_element_type=jnp.float32
        )
        * scale
    )
    all_log, all_delta = (
        lax.all_gather(log_total, "seq", axis=0, tiled=True),
        lax.all_gather(delta, "seq", axis=0, tiled=True),
    )
    query_part = lax.all_gather(query_states, "seq", axis=0, tiled=True)
    grad_part = lax.all_gather(d_attn, "seq", axis=0, tiled=True)
    count = query_part.shape[0]
    query_part = query_part.reshape(count, heads, HD)
    grad_part = grad_part.reshape(count, heads, HD)
    from_rows = block_flags(count, rows, col_allow)
    allowed = from_rows[:, None] | own_sink[None, :]
    scores = (
        jnp.einsum("qhd,khd->qhk", query_part, own_keys, preferred_element_type=jnp.float32) * scale
    )
    probs = jnp.where(allowed[:, None, :], jnp.exp(scores - all_log[..., None]), 0.0)
    dots = jnp.einsum("qhd,khd->qhk", grad_part, own_values, preferred_element_type=jnp.float32)
    grads = probs * (dots - all_delta[..., None])
    key_acc = (
        jnp.einsum(
            "qhk,qhd->khd",
            grads.astype(jnp.bfloat16),
            query_part,
            preferred_element_type=jnp.float32,
        )
        * scale
    )
    value_acc = jnp.einsum(
        "qhk,qhd->khd", probs.astype(jnp.bfloat16), grad_part, preferred_element_type=jnp.float32
    )
    key_acc, value_acc = (key_acc, value_acc)
    return (
        mixed,
        query_grad.astype(jnp.bfloat16).reshape(rows, -1),
        key_acc.astype(jnp.bfloat16).reshape(rows, -1),
        value_acc.astype(jnp.bfloat16).reshape(rows, -1),
    )


def solution(mesh):
    in_specs = (
        P("seq", "head"),
        P("seq", "head"),
        P("seq", "head"),
        P("head", None),
        P(("seq", "head"), None),
        P(),
        P(),
        P(),
    )
    out_specs = (P(("seq", "head"), None), P("seq", "head"), P("seq", "head"), P("seq", "head"))
    return jax.shard_map(
        on_device, mesh=mesh, in_specs=in_specs, out_specs=out_specs, check_vma=False
    )
```

profile of v0, /device:TPU:0, one launch (start us, length us, event | category | flops | bytes accessed | tf_op | source)
XLA Modules:
  0.0 285.5 jit_solution(15006552850157383443)
XLA Ops:
  7.2 0.0 copy-start
  7.2 0.0 all-gather.7.cloned.1.call-start
  7.2 0.7 all-gather.7.cloned.1.call-update
  7.9 0.0 all-gather.5.cloned.1.call-start
  8.0 1.7 copy.45
  9.7 0.0 all-gather.5.cloned.1.call-update
  9.7 0.0 all-gather.9.cloned.1.call-start
  9.8 1.7 copy.46
  11.5 0.0 all-gather.9.cloned.1.call-update
  11.6 0.0 all-gather.11.cloned.1.call-start
  11.6 14.1 %all_gather.25 = bf16[256,1536]{1,0:T(8,128)(2,1)S(1)} all-gather(bf16[64,1536]{1,0:T(8,128)(2,1)} %param.14), channel_id=1, replica_groups=mesh['seq'=32,'head'=4] {'head'}, dimensions={0}, use_global_device_ids=true | all-gather | bytes 983040 | tf_op jit(solution)/shard_map/all_gather | solution.py:66
  25.7 1.3 convolution_convert_fusion.1
  27.0 0.0 all-gather.11.cloned.1.call-update
  27.0 0.0 reduce-scatter.2.cloned.1.call-start
  27.0 1.1 copy.51
  28.1 1.2 dynamic_slice.9
  30.7 1.1 copy.61
  32.4 0.7 dynamic-slice_bitcast_fusion
  33.1 0.7 compare_select_fusion
  33.7 0.7 gather_fusion
  34.4 0.9 dynamic-slice_reduce_fusion
  35.3 0.7 gather_fusion.1
  36.1 0.7 select_compare_fusion.1
  36.7 0.4 fusion.40
  37.1 1.8 fusion.18
  39.0 0.9 compare_reduce_fusion
  39.9 2.6 broadcast_or_fusion
  42.5 19.6 %all-gather.7.cloned.1.call-done = bf16[8192,384]{1,0:T(8,128)(2,1)} async-done(((bf16[256,384]{1,0:T(8,128)(2,1)}), bf16[8192,384]{1,0:T(8,128)(2,1)}) %all-gather.7.cloned.1.call-update) | async-done | bytes 6291472 | tf_op jit(solution)/shard_map/all_gather | solution.py:40
  62.1 8.6 %copy.49 = bf16[8192,384]{0,1:T(8,128)(2,1)} copy(bf16[8192,384]{1,0:T(8,128)(2,1)} %all-gather.7.cloned.1.call-done) | data formatting | bytes 12582912 | tf_op jit(solution)/shard_map/all_gather | solution.py:40
  70.7 47.5 %all-gather.5.cloned.1.call-done = bf16[8192,384]{0,1:T(8,128)(2,1)} async-done(((bf16[256,384]{0,1:T(8,128)(2,1)}), bf16[8192,384]{0,1:T(8,128)(2,1)}) %all-gather.5.cloned.1.call-update) | async-done | bytes 6291472 | tf_op jit(solution)/shard_map/all_gather | solution.py:39
  118.2 13.1 %fusion.8 = (f32[256,3]{0,1:T(4,128)S(1)}, f32[3,8192,256]{2,1,0:T(8,128)}) fusion(pred[8192]{0:T(1024)(128)(4,1)S(1)} %or.25, bf16[8192,3,128]{0,2,1:T(8,128)(2,1)} %bitcast.122, bf16[256,3,128]{0,2,1:T(8,128)(2,1)S(1)} %bitcast.127), kind=kOutput, calls=%fused_computation.16 | convolution fusion | flops 1629486336 | bytes 31665152 | tf_op jit(solution)/shard_map/qhd,khd->qhk/dot_general | solution.py:45
  131.3 12.2 %fusion.9 = f32[256,3]{0,1:T(4,128)S(1)} fusion(f32[3,8192,256]{2,1,0:T(8,128)} %get-tuple-element.22, f32[256,3]{0,1:T(4,128)S(1)} %broadcast_maximum_fusion, pred[8192]{0:T(1024)(128)(4,1)S(1)} %or.25), kind=kLoop, calls=%fused_computation.17 | loop fusion | flops 25165056 | bytes 25180160 | tf_op jit(solution)/shard_map/reduce_sum | solution.py:51
  143.5 3.3 %copy-done.2 = f32[3,8192,256]{2,1,0:T(8,128)S(1)} copy-done((f32[3,8192,256]{2,1,0:T(8,128)S(1)}, f32[3,8192,256]{2,1,0:T(8,128)}, u32[]{:S(2)}) %copy-start.2) | copy-done | bytes 25165848
  146.9 9.4 %multiply_reduce_fusion = (f32[256,3]{0,1:T(4,128)S(1)}, bf16[256,3,128]{0,2,1:T(8,128)(2,1)S(1)}) fusion(bf16[256,3,128]{0,2,1:T(8,128)(2,1)S(1)} %bitcast.130, f32[256,3]{0,1:T(4,128)S(1)} %fusion.9, bf16[8192,3,128]{0,2,1:T(8,128)(2,1)} %bitcast.118, f32[3,8192,256]{2,1,0:T(8,128)S(1)} %copy-done.2, f32[256,3]{0,1:T(4,128)S(1)} %broadcast_maximum_fusion, ...), kind=kOutput, calls=%fused_computation.44 | convolution fusion | flops 1636367616 | bytes 31867904 | tf_op jit(solution)/shard_map/qhk,khd->qhd/dot_general | solution.py:52
  156.3 16.4 %fusion.27 = bf16[3,256,128]{1,2,0:T(8,128)(2,1)S(1)} fusion(bf16[8192,3,128]{0,2,1:T(8,128)(2,1)} %bitcast.123, f32[3,8192,256]{2,1,0:T(8,128)} %get-tuple-element.22, bf16[256,3,128]{0,2,1:T(8,128)(2,1)S(1)} %bitcast.131, bf16[8192,3,128]{0,2,1:T(8,128)(2,1)} %bitcast.119, f32[256,3]{0,1:T(4,128)S(1)} %get-tuple-element.23, ...), kind=kOutput, calls=%fused_computation.35 | convolution fusion | flops 3259170816 | bytes 38156288 | tf_op jit(solution)/shard_map/qhk,khd->qhd/dot_general | solution.py:87
  172.7 0.8 copy.67
  173.5 26.3 %all_gather.29 = f32[8192,3]{0,1:T(4,128)} all-gather(f32[256,3]{0,1:T(4,128)S(1)} %get-tuple-element.23), channel_id=1, replica_groups=mesh['seq'=32,'head'=4] {'seq'}, dimensions={0}, use_global_device_ids=true | all-gather | bytes 101376 | tf_op jit(solution)/shard_map/all_gather | solution.py:94
  199.9 24.5 %all_gather.27 = f32[8192,3]{0,1:T(4,128)} all-gather(f32[256,3]{0,1:T(4,128)S(1)} %log_add_fusion), channel_id=1, replica_groups=mesh['seq'=32,'head'=4] {'seq'}, dimensions={0}, use_global_device_ids=true | all-gather | bytes 101376 | tf_op jit(solution)/shard_map/all_gather | solution.py:93
  224.4 1.5 convolution_convert_fusion
  225.9 0.0 reduce-scatter.2.cloned.1.call-update
  225.9 0.0 all-gather.9.cloned.1.call-done
  225.9 13.0 %fusion.52 = f32[3,256,8192]{2,1,0:T(8,128)} fusion(bf16[256,3,128]{0,2,1:T(8,128)(2,1)S(1)} %bitcast.126, bf16[8192,3,128]{0,2,1:T(8,128)(2,1)} %bitcast.124), kind=kOutput, calls=%fused_computation.71 | convolution fusion | flops 1610612736 | bytes 31653888 | tf_op jit(solution)/shard_map/qhd,khd->qhk/dot_general | solution.py:104
  239.0 0.0 all-gather.11.cloned.1.call-done
  239.0 8.8 %copy.60 = bf16[8192,384]{0,1:T(8,128)(2,1)} copy(bf16[8192,384]{1,0:T(8,128)(2,1)} %all-gather.11.cloned.1.call-done) | data formatting | bytes 12582912 | tf_op jit(solution)/shard_map/all_gather | solution.py:97
  247.8 16.3 %fusion.26 = bf16[3,256,128]{1,2,0:T(8,128)(2,1)S(1)} fusion(bf16[8192,3,128]{0,2,1:T(8,128)(2,1)} %bitcast.125, f32[3,256,8192]{2,1,0:T(8,128)} %fusion.52, bf16[8192,3,128]{0,2,1:T(8,128)(2,1)} %bitcast.120, bf16[256,3,128]{0,2,1:T(8,128)(2,1)S(1)} %bitcast.129, f32[8192,3]{0,1:T(4,128)S(1)} %copy-done.7, f32[8192,3]{0,1:T(4,128)S(1)} %copy-done.6, ...), kind=kOutput, calls=%fused_computation.34 | convolution fusion | flops 3259170816 | bytes 40435712 | tf_op jit(solution)/shard_map/qhk,qhd->khd/dot_general | solution.py:110
  264.1 0.8 copy.68
  264.9 13.2 %fusion.28 = bf16[3,128,256]{2,1,0:T(8,128)(2,1)S(1)} fusion(bf16[8192,3,128]{0,2,1:T(8,128)(2,1)} %bitcast.121, f32[3,256,8192]{2,1,0:T(8,128)} %fusion.52, f32[8192,3]{0,1:T(4,128)} %all_gather.27, pred[8192,256]{0,1:T(8,128)(4,1)S(1)} %copy-done.3), kind=kOutput, calls=%fused_computation.36 | convolution fusion | flops 1635876864 | bytes 33849344 | tf_op jit(solution)/shard_map/qhk,qhd->khd/dot_general | solution.py:118
  278.2 0.8 copy.69
  (21 shorter events, 0.1 us)
Async XLA Ops:
  7.2 18.5 %copy-start = (bf16[384,1536]{1,0:T(8,128)(2,1)S(1)}, bf16[384,1536]{1,0:T(8,128)(2,1)}, u32[]{:S(2)}) copy-start(bf16[384,1536]{1,0:T(8,128)(2,1)} %param.13) | copy-start | bytes 3538948
  7.2 54.9 %all-gather.7.cloned.1.call-start = ((), (), s32[]{:S(2)}) async-start(), calls=%async_computation.2 | async-start | bytes 6488064 | tf_op jit(solution)/shard_map/all_gather | solution.py:40
  7.9 110.3 %all-gather.5.cloned.1.call-start = ((), (), s32[]{:S(2)}) async-start(), calls=%async_computation.1 | async-start | bytes 6488064 | tf_op jit(solution)/shard_map/all_gather | solution.py:39
  9.7 216.2 %all-gather.9.cloned.1.call-start = ((), (), s32[]{:S(2)}) async-start(), calls=%async_computation.4 | async-start | bytes 6488064 | tf_op jit(solution)/shard_map/all_gather | solution.py:96
  11.5 106.7 %copy-start.5 = (bf16[256,384]{0,1:T(8,128)(2,1)S(1)}, bf16[256,384]{0,1:T(8,128)(2,1)}, u32[]{:S(2)}) copy-start(bf16[256,384]{0,1:T(8,128)(2,1)} %copy.46) | copy-start | bytes 589828
  11.6 227.4 %all-gather.11.cloned.1.call-start = ((), (), s32[]{:S(2)}) async-start(), calls=%async_computation.5 | async-start | bytes 6488064 | tf_op jit(solution)/shard_map/all_gather | solution.py:97
  27.0 252.0 %reduce-scatter.2.cloned.1.call-start = ((), (), s32[]{:S(2)}) async-start(), calls=%async_computation.3 | async-start | bytes 983040 | tf_op jit(solution)/shard_map/reduce_scatter | solution.py:59
  131.3 15.5 %copy-start.2 = (f32[3,8192,256]{2,1,0:T(8,128)S(1)}, f32[3,8192,256]{2,1,0:T(8,128)}, u32[]{:S(2)}) copy-start(f32[3,8192,256]{2,1,0:T(8,128)} %get-tuple-element.22) | copy-start | bytes 75497472
  156.3 69.7 %copy-start.4 = (bf16[256,384]{0,1:T(8,128)(2,1)S(1)}, bf16[256,384]{0,1:T(8,128)(2,1)}, u32[]{:S(2)}) copy-start(bf16[256,384]{0,1:T(8,128)(2,1)} %copy.45) | copy-start | bytes 589828
  239.0 8.8 %copy-start.3 = (pred[8192,256]{0,1:T(8,128)(4,1)S(1)}, pred[8192,256]{0,1:T(8,128)(4,1)}, u32[]{:S(2)}) copy-start(pred[8192,256]{0,1:T(8,128)(4,1)} %broadcast_or_fusion) | copy-start | bytes 6291460
  239.0 8.8 %copy-start.6 = (f32[8192,3]{0,1:T(4,128)S(1)}, f32[8192,3]{0,1:T(4,128)}, u32[]{:S(2)}) copy-start(f32[8192,3]{0,1:T(4,128)} %all_gather.27) | copy-start | bytes 294916
  239.0 8.8 %copy-start.7 = (f32[8192,3]{0,1:T(4,128)S(1)}, f32[8192,3]{0,1:T(4,128)}, u32[]{:S(2)}) copy-start(f32[8192,3]{0,1:T(4,128)} %all_gather.29) | copy-start | bytes 294916
  264.9 14.0 %copy-start.1 = (bf16[384,1536]{1,0:T(8,128)(2,1)S(1)}, bf16[384,1536]{1,0:T(8,128)(2,1)}, u32[]{:S(2)}) copy-start(bf16[384,1536]{1,0:T(8,128)(2,1)} %param.13) | copy-start | bytes 3538948
Sparse Core Ops, SparseCore 0:
  10.3 51.7 all-gather.6
  64.8 53.3 all-gather.4
  120.4 54.0 all-gather.8
  177.2 49.2 all-gather.10
  229.3 21.0 reduce-scatter.1
where the time goes:
time: 288 us; the launch traced here: 286 us
  matrix products  84.3 us (29%)
  waiting for transfers between devices  67.9 us (24%)
  blocking collectives  65 us (23%)
  local copies, waits for them, and re-layouts  33.1 us (11%)
  other arithmetic  19.2 us (7%)
  between operations  15.9 us (6%)
    all_gather x1, waiting for transfers between devices, on_device(): key_part = lax.all_gather(key_states, 'seq', axis=0, tiled=True)  47.5 us
    all_gather x1, blocking collectives, on_device(): lax.all_gather(delta, 'seq', axis=0, tiled=True)  26.3 us
    all_gather x1, blocking collectives, on_device(): lax.all_gather(log_total, 'seq', axis=0, tiled=True)  24.5 us
    all_gather x1, waiting for transfers between devices, on_device(): value_part = lax.all_gather(value_states, 'seq', axis=0, tiled=True)  19.6 us
    dot_general x1, matrix products, on_device(): jnp.einsum('qhk,khd->qhd', grads.astype(jnp.bfloat16), key_part, preferre...  16.4 us
    dot_general x1, matrix products, on_device(): jnp.einsum('qhk,qhd->khd', grads.astype(jnp.bfloat16), query_part, prefer...  16.3 us
    all_gather x1, blocking collectives, on_device(): lax.all_gather(out_grad, 'head', axis=0, tiled=True)  14.1 us
    dot_general x1, matrix products, on_device(): jnp.einsum('qhk,qhd->khd', probs.astype(jnp.bfloat16), grad_part, preferr...  13.2 us
  transfers between devices with their start and end apart: 5, of which 2 were waited for; matrix products, arithmetic and copies ran while one was open for 47% of the time, Pallas kernels for 0%

commit v1 on v0

v1 whole, which is shorter than its diff:
```python
import jax
import jax.numpy as jnp
from jax import lax
from jax.experimental import pallas as pl
from jax.experimental.pallas import tpu as pltpu
from jax.sharding import PartitionSpec as P

HD = 128
ROWS = 256
HEADS = 3
NQ = 4
NK = 8
QN = NQ * ROWS
KN = NK * ROWS
SCALE = HD ** (-0.5)
LOG2E = 1.4426950408889634
C2 = SCALE * LOG2E
NEG = -1e30
MESH = pl.DeviceIdType.MESH
f32 = jnp.float32
bf16 = jnp.bfloat16


def dot(a, b, left, right):
    return lax.dot_general(a, b, (((left,), (right,)), ((), ())), preferred_element_type=f32)


def slot_of(core, step):
    return core * 4 + (step + 3) % 4


def kernel(
    q_in, k_in, v_in, w_in, g_in, place, sinks, table,
    mixed_out, dq_out, dk_out, dv_out,
    qg, dog, kg, vg, wts, s_buf, kaug, qaug, ow, og, o_t, st, attn,
    o_send, o_recv, dq_send, dq_recv, sib_send, sib_recv, z_send, z_recv, own_kv, m_send, m_recv,
    local_sem, q_ss, q_rs, kv_ss, kv_rs, fw_ss, fw_rs, x_ss, x_rs, do_ss, do_rs, st_ss, st_rs,
    o_ss, o_rs, dq_ss, dq_rs, sg_ss, sg_rs, zg_ss, zg_rs, m_ss, m_rs,
):
    s = lax.axis_index("seq")
    x = lax.axis_index("head")
    c = lax.rem(s, 2)
    y = lax.rem(s // 2, 4)
    z = s // 8

    def y_peer(d):
        return {"seq": (z * 4 + lax.rem(y + d, 4)) * 2 + c}

    def z_peer(d):
        return {"seq": (lax.rem(z + d, 4) * 4 + y) * 2 + c}

    def x_peer(d):
        return {"head": lax.rem(x + d, 4)}

    sibling = {"seq": s + 1 - 2 * c}

    def remote(src, dst, send_sem, recv_sem, peer):
        return pltpu.make_async_remote_copy(
            src_ref=src, dst_ref=dst, send_sem=send_sem, recv_sem=recv_sem, device_id=peer, device_id_type=MESH
        )

    def cols(h):
        return pl.ds(h * HD, HD)

    local = [pltpu.make_async_copy(g_in, og.at[x], local_sem.at[0]), pltpu.make_async_copy(w_in, ow, local_sem.at[1])]
    for h in range(HEADS):
        local.append(pltpu.make_async_copy(q_in.at[:, cols(h)], qg.at[h, y], local_sem.at[2 + h]))
        local.append(pltpu.make_async_copy(k_in.at[:, cols(h)], kg.at[h, slot_of(0, 0)], local_sem.at[5 + h]))
        local.append(pltpu.make_async_copy(v_in.at[:, cols(h)], vg.at[h, slot_of(0, 0)], local_sem.at[8 + h]))
    for copy in local:
        copy.start()

    peers = [y_peer(1), y_peer(2), y_peer(3), z_peer(1), z_peer(2), z_peer(3), x_peer(1), x_peer(2), x_peer(3), sibling]
    barrier = pltpu.get_barrier_semaphore()
    for peer in peers:
        pl.semaphore_signal(barrier, inc=1, device_id=peer, device_id_type=MESH)
    pl.semaphore_wait(barrier, len(peers))

    x_copies = [remote(g_in, og.at[x], x_ss.at[d - 1], x_rs.at[d - 1], x_peer(d)) for d in (1, 2, 3)]
    q_copies, kv_copies, fw_copies = [], {}, {}
    for copy in x_copies:
        copy.start()
    for h in range(HEADS):
        q_copies.append([
            remote(q_in.at[:, cols(h)], qg.at[h, y], q_ss.at[h, d - 1], q_rs.at[h, d - 1], y_peer(d)) for d in (1, 3, 2)
        ])
    for n, (src, dst) in enumerate(((k_in, kg), (v_in, vg))):
        for h in range(HEADS):
            kv_copies[n, h] = [
                remote(
                    src.at[:, cols(h)], dst.at[h, slot_of(0, 4 - d)], kv_ss.at[n, h, d - 1], kv_rs.at[n, h, d - 1], z_peer(d)
                )
                for d in (1, 3, 2)
            ]
            fw_copies[n, h] = [
                remote(
                    src.at[:, cols(h)] if d == 0 else dst.at[h, slot_of(0, 4 - d)],
                    dst.at[h, slot_of(1, (4 - d) % 4)],
                    fw_ss.at[n, h, d], fw_rs.at[n, h, d], sibling,
                )
                for d in (0, 1, 3, 2)
            ]
    for h in range(HEADS):
        for a, b in zip(kv_copies[0, h], q_copies[h]):
            a.start()
            b.start()
        fw_copies[0, h][0].start()
    for h in range(HEADS):
        for a in kv_copies[1, h]:
            a.start()
        fw_copies[1, h][0].start()

    lane = lax.broadcasted_iota(jnp.int32, (1, HD), 1)
    q_spans = [place[(z * 4 + j) * 2 + c] for j in range(NQ)]
    row = lax.broadcasted_iota(jnp.int32, (ROWS, sinks.shape[1]), 0)
    ids = sinks[...]
    for core in range(2):
        for step in range(4):
            block = (lax.rem(z + step, 4) * 4 + y) * 2 + (c if core == 0 else 1 - c)
            span = place[block]
            bias = jnp.zeros((1, HD), f32)
            for j in range(NQ):
                barred = (1 - table[q_spans[j], span]).astype(f32) * NEG
                bias = bias + jnp.where(lane == j, barred, 0.0)
            sink = jnp.max(jnp.where(row + block * ROWS == ids, 1.0, 0.0), axis=1, keepdims=True)
            kaug[slot_of(core, step)] = jnp.where(sink > 0.5, 0.0, bias).astype(bf16)
    for j in range(NQ):
        qaug[j] = jnp.broadcast_to(jnp.where(lane == j, 1.0, 0.0), (ROWS, HD)).astype(bf16)

    def forward_keys(n, h):
        for a, b in zip(kv_copies[n, h], fw_copies[n, h][1:]):
            a.wait_recv()
            b.start()
        for b in fw_copies[n, h]:
            b.wait_recv()

    def scores(h):
        def one(j, carry):
            queries = jnp.concatenate([qg[h, j], qaug[j]], axis=1)
            half = pl.ds(pl.multiple_of(lax.rem(j, 2) * ROWS, ROWS), ROWS)
            mine = pl.ds(pl.multiple_of(j * ROWS, ROWS), ROWS)
            top = jnp.full((8, ROWS), -jnp.inf, f32)
            for i in range(NK):
                keys = jnp.concatenate([kg[h, i], kaug[i]], axis=1)
                t = dot(keys, queries, 1, 1)
                s_buf[pl.ds(i * ROWS, ROWS), half] = t
                top = jnp.maximum(top, jnp.max(t.reshape(ROWS // 8, 8, ROWS), axis=0))
            m = jnp.max(top, axis=0, keepdims=True) * C2
            total = jnp.zeros((8, ROWS), f32)
            for i in range(NK):
                w = jnp.exp2(s_buf[pl.ds(i * ROWS, ROWS), half] * C2 - m)
                wts[h, pl.ds(i * ROWS, ROWS), mine] = w.astype(bf16)
                total = total + jnp.sum(w.reshape(ROWS // 8, 8, ROWS), axis=0)
            st[h, y, pl.ds(j, 1), :] = m
            st[h, y, pl.ds(NQ + j, 1), :] = jnp.sum(total, axis=0, keepdims=True)
            return carry

        lax.fori_loop(0, NQ, one, 0, unroll=True)

    def weigh(h):
        for j in range(NQ):
            mine = pl.ds(j * ROWS, ROWS)
            o_t[h, :, mine] = dot(vg[h].reshape(KN, HD), wts[h, :, mine], 0, 0)

    def deltas(h):
        for j in range(NQ):
            prod = o_t[h, :, pl.ds(j * ROWS, ROWS)] * dog[h, j].astype(f32).T
            st[h, y, pl.ds(2 * NQ + j, 1), :] = jnp.sum(prod, axis=0, keepdims=True)

    def combine(h):
        ms = [st[h, g, pl.ds(0, NQ), :] for g in range(4)]
        top = jnp.maximum(jnp.maximum(ms[0], ms[1]), jnp.maximum(ms[2], ms[3]))
        es = [jnp.exp2(m - top) for m in ms]
        total = sum(e * st[h, g, pl.ds(NQ, NQ), :] for g, e in enumerate(es))
        summed = sum(e * st[h, g, pl.ds(2 * NQ, NQ), :] for g, e in enumerate(es))
        factor = jnp.exp2(st[h, y, pl.ds(0, NQ), :] - top) / total
        return factor, summed / total

    def as_row(a):
        return jnp.concatenate([a[j : j + 1] for j in range(NQ)], axis=1)

    for copy in local:
        copy.wait()
    for h in range(HEADS):
        for copy in q_copies[h]:
            copy.wait_recv()
        forward_keys(0, h)
        scores(h)

    for copy in x_copies:
        copy.wait_recv()
    do_copies = []
    for h in range(HEADS):
        d_attn = dot(og[...].reshape(ROWS, og.shape[2]), ow[cols(h), :], 1, 1)
        dog[h, y] = d_attn.astype(bf16)
        do_copies.append([
            remote(dog.at[h, y], dog.at[h, y], do_ss.at[h, d - 1], do_rs.at[h, d - 1], y_peer(d)) for d in (1, 3, 2)
        ])
        for copy in do_copies[h]:
            copy.start()

    for h in range(HEADS):
        forward_keys(1, h)
        weigh(h)

    st_copies = []
    for h in range(HEADS):
        for copy in do_copies[h]:
            copy.wait_recv()
        deltas(h)
        st_copies.append([
            remote(st.at[h, y], st.at[h, y], st_ss.at[h, d - 1], st_rs.at[h, d - 1], y_peer(d)) for d in (1, 3, 2)
        ])
        for copy in st_copies[h]:
            copy.start()

    factors, delta_rows, o_copies = [], [], []
    for h in range(HEADS):
        for copy in st_copies[h]:
            copy.wait_recv()
        factor, delta = combine(h)
        factors.append(as_row(factor))
        delta_rows.append(as_row(delta))
        for j in range(NQ):
            o_send[h, j] = (o_t[h, :, pl.ds(j * ROWS, ROWS)] * factor[j : j + 1]).T.astype(bf16)
        o_copies.append([
            remote(o_send.at[h, lax.rem(y + d, 4)], o_recv.at[h, d - 1], o_ss.at[h, d - 1], o_rs.at[h, d - 1], y_peer(d))
            for d in (1, 3, 2)
        ])
        for copy in o_copies[h]:
            copy.start()

    sg_copies, zg_copies, dq_copies = {}, {}, []

    def backward(h):
        factor, delta = factors[h], delta_rows[h]
        queries = qg[h].reshape(QN, HD)
        cots = dog[h].reshape(QN, HD)
        dq = jnp.zeros((HD, QN), f32)
        for t, first in enumerate((4, 6, 0, 2)):
            rows = pl.ds(first * ROWS, 2 * ROWS)
            keys = kg[h, pl.ds(first, 2)].reshape(2 * ROWS, HD)
            values = vg[h, pl.ds(first, 2)].reshape(2 * ROWS, HD)
            dots = dot(values, cots, 1, 1)
            probs = wts[h, rows, :].astype(f32) * factor
            grads = (probs * (dots - delta)).astype(bf16)
            dv = dot(probs.astype(bf16), cots, 1, 0)
            dk = dot(grads, queries, 1, 0) * SCALE
            dq = dq + dot(keys, grads, 0, 0)
            if first >= 4:
                for i in range(2):
                    sib_send[h, first - 4 + i, 0] = dk[i * ROWS : (i + 1) * ROWS].astype(bf16)
                    sib_send[h, first - 4 + i, 1] = dv[i * ROWS : (i + 1) * ROWS].astype(bf16)
                part = pl.ds(first - 4, 2)
                sg_copies[h, t] = remote(
                    sib_send.at[h, part], sib_recv.at[h, part], sg_ss.at[h, t], sg_rs.at[h, t], sibling
                )
                sg_copies[h, t].start()
            else:
                sg_copies[h, t - 2].wait_recv()
                for i in range(2):
                    slot = first + i
                    step = (slot + 1) % 4
                    for n, grad in enumerate((dk, dv)):
                        both = grad[i * ROWS : (i + 1) * ROWS] + sib_recv[h, slot, n].astype(f32)
                        if step == 0:
                            own_kv[h, n] = both
                        else:
                            z_send[h, step - 1, n] = both.astype(bf16)
                    if step != 0:
                        zg_copies[h, step] = remote(
                            z_send.at[h, step - 1], z_recv.at[h, step - 1], zg_ss.at[h, step - 1], zg_rs.at[h, step - 1],
                            z_peer(step),
                        )
                        zg_copies[h, step].start()
        for j in range(NQ):
            dq_send[h, j] = (dq[:, j * ROWS : (j + 1) * ROWS] * SCALE).T.astype(bf16)
        dq_copies.append([
            remote(dq_send.at[h, lax.rem(y + d, 4)], dq_recv.at[h, d - 1], dq_ss.at[h, d - 1], dq_rs.at[h, d - 1], y_peer(d))
            for d in (1, 3, 2)
        ])
        for copy in dq_copies[h]:
            copy.start()

    def finish(h):
        for copy in dq_copies[h]:
            copy.wait_recv()
        dq = dq_send[h, y].astype(f32)
        for i in range(3):
            dq = dq + dq_recv[h, i].astype(f32)
        dq_out[:, cols(h)] = dq.astype(bf16)
        for step in (1, 2, 3):
            zg_copies[h, step].wait_recv()
        for n, out in enumerate((dk_out, dv_out)):
            total = own_kv[h, n]
            for i in range(3):
                total = total + z_recv[h, i, n].astype(f32)
            out[:, cols(h)] = total.astype(bf16)

    backward(0)
    backward(1)

    for h in range(HEADS):
        for copy in o_copies[h]:
            copy.wait_recv()
        total = o_send[h, y].astype(f32)
        for i in range(3):
            total = total + o_recv[h, i].astype(f32)
        attn[:, cols(h)] = total.astype(bf16)
    m_send[...] = dot(attn[...], ow[...], 1, 0).astype(bf16).reshape(m_send.shape)
    m_copies = [
        remote(m_send.at[lax.rem(x + d, 4)], m_recv.at[d - 1], m_ss.at[d - 1], m_rs.at[d - 1], x_peer(d)) for d in (1, 3, 2)
    ]
    for copy in m_copies:
        copy.start()

    backward(2)
    finish(0)
    finish(1)
    for copy in m_copies:
        copy.wait_recv()
    mixed = m_send[x].astype(f32)
    for i in range(3):
        mixed = mixed + m_recv[i].astype(f32)
    mixed_out[...] = mixed.astype(bf16)
    finish(2)

    for copy in x_copies + m_copies:
        copy.wait_send()
    for group in q_copies + do_copies + st_copies + o_copies + dq_copies + list(kv_copies.values()) + list(fw_copies.values()):
        for copy in group:
            copy.wait_send()
    for copy in list(sg_copies.values()) + list(zg_copies.values()):
        copy.wait_send()


def on_device(
    query_states, key_states, value_states, out_weight, out_grad, placement, sink_ids, span_mask
):
    width = out_weight.shape[1]
    part = out_grad.shape[0]
    vmem = pl.BlockSpec(memory_space=pltpu.VMEM)
    smem = pl.BlockSpec(memory_space=pltpu.SMEM)
    hbm = pl.BlockSpec(memory_space=pl.ANY)
    own = (ROWS, HEADS * HD)

    def sem(*shape):
        return pltpu.SemaphoreType.DMA(shape)

    scratch = [
        pltpu.VMEM((HEADS, NQ, ROWS, HD), bf16),
        pltpu.VMEM((HEADS, NQ, ROWS, HD), bf16),
        pltpu.VMEM((HEADS, NK, ROWS, HD), bf16),
        pltpu.VMEM((HEADS, NK, ROWS, HD), bf16),
        pltpu.VMEM((HEADS, KN, QN), bf16),
        pltpu.VMEM((KN, 2 * ROWS), f32),
        pltpu.VMEM((NK, ROWS, HD), bf16),
        pltpu.VMEM((NQ, ROWS, HD), bf16),
        pltpu.VMEM((HEADS * HD, width), bf16),
        pltpu.VMEM((4, part, width), bf16),
        pltpu.VMEM((HEADS, HD, QN), f32),
        pltpu.VMEM((HEADS, 4, 16, ROWS), f32),
        pltpu.VMEM(own, bf16),
        pltpu.VMEM((HEADS, NQ, ROWS, HD), bf16),
        pltpu.VMEM((HEADS, 3, ROWS, HD), bf16),
        pltpu.VMEM((HEADS, NQ, ROWS, HD), bf16),
        pltpu.VMEM((HEADS, 3, ROWS, HD), bf16),
        pltpu.VMEM((HEADS, 4, 2, ROWS, HD), bf16),
        pltpu.VMEM((HEADS, 4, 2, ROWS, HD), bf16),
        pltpu.VMEM((HEADS, 3, 2, ROWS, HD), bf16),
        pltpu.VMEM((HEADS, 3, 2, ROWS, HD), bf16),
        pltpu.VMEM((HEADS, 2, ROWS, HD), f32),
        pltpu.VMEM((4, part, width), bf16),
        pltpu.VMEM((3, part, width), bf16),
        sem(11),
        sem(HEADS, 3), sem(HEADS, 3),
        sem(2, HEADS, 3), sem(2, HEADS, 3),
        sem(2, HEADS, 4), sem(2, HEADS, 4),
        sem(3), sem(3),
        sem(HEADS, 3), sem(HEADS, 3),
        sem(HEADS, 3), sem(HEADS, 3),
        sem(HEADS, 3), sem(HEADS, 3),
        sem(HEADS, 3), sem(HEADS, 3),
        sem(HEADS, 2), sem(HEADS, 2),
        sem(HEADS, 3), sem(HEADS, 3),
        sem(3), sem(3),
    ]
    return pl.pallas_call(
        kernel,
        out_shape=[jax.ShapeDtypeStruct((part, width), bf16)] + [jax.ShapeDtypeStruct(own, bf16)] * 3,
        in_specs=[hbm] * 5 + [smem, vmem, smem],
        out_specs=[vmem] * 4,
        scratch_shapes=scratch,
        compiler_params=pltpu.CompilerParams(
            collective_id=0, has_side_effects=True, vmem_limit_bytes=56 * 2**20
        ),
        name="attention",
    )(
        query_states, key_states, value_states, out_weight, out_grad,
        placement, sink_ids.reshape(1, -1), span_mask,
    )


def solution(mesh):
    in_specs = (
        P("seq", "head"),
        P("seq", "head"),
        P("seq", "head"),
        P("head", None),
        P(("seq", "head"), None),
        P(),
        P(),
        P(),
    )
    out_specs = (P(("seq", "head"), None), P("seq", "head"), P("seq", "head"), P("seq", "head"))
    return jax.shard_map(
        on_device, mesh=mesh, in_specs=in_specs, out_specs=out_specs, check_vma=False
    )
```

time: 288 us -> 75 us (0.26)
  matrix products: 84.3 us -> 0 us
  Pallas kernels: 0 us -> 68.3 us
  waiting for transfers between devices: 67.9 us -> 0 us
  blocking collectives: 65 us -> 0 us
  local copies, waits for them, and re-layouts: 33.1 us -> 5.58 us
  other arithmetic: 19.2 us -> 0 us
  between operations: 15.9 us -> 0.65 us
    dot_general x8 -> x0, matrix products: 84.3 us -> none  [the longest x1 16.4 us: on_device(): jnp.einsum('qhk,khd->qhd', grads.astype(jnp.bfloat16), key_part, preferre...]
    pallas_call x0 -> x1, Pallas kernels: none -> 68.3 us  [on_device(): pl.pallas_call(kernel, out_shape=[jax.ShapeDtypeStruct((part, width), bf1...]
    all_gather x4 -> x0, waiting for transfers between devices: 67.2 us -> none  [the longest x1 47.5 us: on_device(): key_part = lax.all_gather(key_states, 'seq', axis=0, tiled=True)]
    all_gather x3 -> x0, blocking collectives: 65 us -> none  [the longest x1 26.3 us: on_device(): lax.all_gather(delta, 'seq', axis=0, tiled=True)]
    all_gather x2 -> x0, local copies, waits for them, and re-layouts: 17.4 us -> none  [the longest x1 8.79 us: on_device(): grad_part = lax.all_gather(d_attn, 'seq', axis=0, tiled=True)]
    reduce_sum x1 -> x0, other arithmetic: 12.2 us -> none  [on_device(): total = jnp.sum(weights, axis=-1)]
    unnamed x22 -> x6, local copies, waits for them, and re-layouts: 10.4 us -> 5.58 us
    reduce_or x3 -> x0, other arithmetic: 3.12 us -> none  [the longest x1 1.84 us: sink_flags(): return jnp.any(positions[:, None] == sink_ids[None, :], axis=1)]
  transfers between devices with their start and end apart: 5 -> 0, of which waited for: 2 -> 0; matrix products, arithmetic and copies ran while one was open for 47% -> 0% of each run, Pallas kernels for 0% -> 0%
where the time goes in v1:
time: 75 us; the launch traced here: 74.6 us
  Pallas kernels  68.3 us (91%)
  local copies, waits for them, and re-layouts  5.58 us (7%)
    pallas_call x1, Pallas kernels, on_device(): pl.pallas_call(kernel, out_shape=[jax.ShapeDtypeStruct((part, width), bf1...  68.3 us
    unnamed x6, local copies, waits for them, and re-layouts  5.58 us

profile of v1, /device:TPU:0, one launch (start us, length us, event | category | flops | bytes accessed | tf_op | source)
XLA Modules:
  0.0 74.6 jit_solution(12488690161961804246)
XLA Ops:
  0.6 68.3 %attention.1 = (bf16[64,1536]{1,0:T(8,128)(2,1)}, bf16[256,384]{1,0:T(8,128)(2,1)}, bf16[256,384]{1,0:T(8,128)(2,1)}, bf16[256,384]{1,0:T(8,128)(2,1)}) custom-call(bf16[256,384]{1,0:T(8,128)(2,1)} %q_in.1, bf16[256,384]{1,0:T(8,128)(2,1)} %k_in.1, bf16[256,384]{1,0:T(8,128)(2,1)} %v_in.1, bf16[384,1536]{1,0:T(8,128)(2,1)} %w_in.1, bf16[64,1536]{1,0:T(8,128)(2,1)} %g_in.1, ...), custom_call_target="tpu_custom_call" | custom-call | tf_op jit(solution)/shard_map/attention/pallas_call | solution.py:388
  69.0 0.0 copy-start
  69.0 1.7 %copy.16 = bf16[64,1536]{1,0:T(8,128)(2,1)} copy(bf16[64,1536]{1,0:T(8,128)(2,1)} %get-tuple-element.8) | data formatting | bytes 393216
  70.7 1.6 %copy.17 = bf16[256,384]{1,0:T(8,128)(2,1)} copy(bf16[256,384]{1,0:T(8,128)(2,1)} %get-tuple-element.9) | data formatting | bytes 393216
  72.3 1.6 %copy.18 = bf16[256,384]{1,0:T(8,128)(2,1)} copy(bf16[256,384]{1,0:T(8,128)(2,1)} %get-tuple-element.10) | data formatting | bytes 393216
  73.9 0.0 copy-done
  73.9 0.7 copy.19
Async XLA Ops:
  69.0 4.9 %copy-start = (bf16[256,384]{1,0:T(8,128)(2,1)S(1)}, bf16[256,384]{1,0:T(8,128)(2,1)}, u32[]{:S(2)}) copy-start(bf16[256,384]{1,0:T(8,128)(2,1)} %get-tuple-element.11) | copy-start | bytes 589828

commit v2 on v1

--- a/solution.py
+++ b/solution.py
@@ -32,10 +32,10 @@
 def kernel(
     q_in, k_in, v_in, w_in, g_in, place, sinks, table,
     mixed_out, dq_out, dk_out, dv_out,
-    qg, dog, kg, vg, wts, s_buf, kaug, qaug, ow, og, o_t, st, attn,
-    o_send, o_recv, dq_send, dq_recv, sib_send, sib_recv, z_send, z_recv, own_kv, m_send, m_recv,
+    qg, dog, kg, vg, wts, s_buf, kaug, qaug, ow, og, o_t, st, dl, attn,
+    o_send, o_recv, dq_send, dq_recv, sib_send, sib_recv, z_send, z_recv, part_kv, m_send, m_recv,
     local_sem, q_ss, q_rs, kv_ss, kv_rs, fw_ss, fw_rs, x_ss, x_rs, do_ss, do_rs, st_ss, st_rs,
-    o_ss, o_rs, dq_ss, dq_rs, sg_ss, sg_rs, zg_ss, zg_rs, m_ss, m_rs,
+    d_ss, d_rs, o_ss, o_rs, dq_ss, dq_rs, sg_ss, sg_rs, zg_ss, zg_rs, m_ss, m_rs,
 ):
     s = lax.axis_index("seq")
     x = lax.axis_index("head")
@@ -76,7 +76,7 @@
         pl.semaphore_signal(barrier, inc=1, device_id=peer, device_id_type=MESH)
     pl.semaphore_wait(barrier, len(peers))
 
-    x_copies = [remote(g_in, og.at[x], x_ss.at[d - 1], x_rs.at[d - 1], x_peer(d)) for d in (1, 2, 3)]
+    x_copies = [remote(g_in, og.at[x], x_ss.at[d - 1], x_rs.at[d - 1], x_peer(d)) for d in (1, 3, 2)]
     q_copies, kv_copies, fw_copies = [], {}, {}
     for copy in x_copies:
         copy.start()
@@ -127,12 +127,26 @@
     for j in range(NQ):
         qaug[j] = jnp.broadcast_to(jnp.where(lane == j, 1.0, 0.0), (ROWS, HD)).astype(bf16)
 
-    def forward_keys(n, h):
+    def forward(n, h):
         for a, b in zip(kv_copies[n, h], fw_copies[n, h][1:]):
             a.wait_recv()
             b.start()
+
+    def await_forwarded(n, h):
         for b in fw_copies[n, h]:
             b.wait_recv()
+
+    def share(buf, send_sems, recv_sems, h):
+        copies = [
+            remote(buf.at[h, y], buf.at[h, y], send_sems.at[h, d - 1], recv_sems.at[h, d - 1], y_peer(d)) for d in (1, 3, 2)
+        ]
+        for copy in copies:
+            copy.start()
+        return copies
+
+    def await_all(copies):
+        for copy in copies:
+            copy.wait_recv()
 
     def scores(h):
         def one(j, carry):
@@ -158,121 +172,105 @@
         lax.fori_loop(0, NQ, one, 0, unroll=True)
 
     def weigh(h):
-        for j in range(NQ):
-            mine = pl.ds(j * ROWS, ROWS)
+        for j in range(NQ // 2):
+            mine = pl.ds(j * 2 * ROWS, 2 * ROWS)
             o_t[h, :, mine] = dot(vg[h].reshape(KN, HD), wts[h, :, mine], 0, 0)
-
-    def deltas(h):
-        for j in range(NQ):
-            prod = o_t[h, :, pl.ds(j * ROWS, ROWS)] * dog[h, j].astype(f32).T
-            st[h, y, pl.ds(2 * NQ + j, 1), :] = jnp.sum(prod, axis=0, keepdims=True)
 
     def combine(h):
         ms = [st[h, g, pl.ds(0, NQ), :] for g in range(4)]
         top = jnp.maximum(jnp.maximum(ms[0], ms[1]), jnp.maximum(ms[2], ms[3]))
-        es = [jnp.exp2(m - top) for m in ms]
-        total = sum(e * st[h, g, pl.ds(NQ, NQ), :] for g, e in enumerate(es))
-        summed = sum(e * st[h, g, pl.ds(2 * NQ, NQ), :] for g, e in enumerate(es))
-        factor = jnp.exp2(st[h, y, pl.ds(0, NQ), :] - top) / total
-        return factor, summed / total
+        total = sum(jnp.exp2(m - top) * st[h, g, pl.ds(NQ, NQ), :] for g, m in enumerate(ms))
+        return jnp.exp2(st[h, y, pl.ds(0, NQ), :] - top) / total
+
+    def deltas(h, factor):
+        for j in range(NQ):
+            part = o_t[h, :, pl.ds(j * ROWS, ROWS)] * factor[j : j + 1]
+            o_send[h, j] = part.T.astype(bf16)
+            dl[h, y, pl.ds(j, 1), :] = jnp.sum(part * cotangents(j, h).astype(f32).T, axis=0, keepdims=True)
 
     def as_row(a):
         return jnp.concatenate([a[j : j + 1] for j in range(NQ)], axis=1)
 
-    for copy in local:
-        copy.wait()
-    for h in range(HEADS):
-        for copy in q_copies[h]:
-            copy.wait_recv()
-        forward_keys(0, h)
-        scores(h)
-
-    for copy in x_copies:
-        copy.wait_recv()
-    do_copies = []
-    for h in range(HEADS):
-        d_attn = dot(og[...].reshape(ROWS, og.shape[2]), ow[cols(h), :], 1, 1)
-        dog[h, y] = d_attn.astype(bf16)
-        do_copies.append([
-            remote(dog.at[h, y], dog.at[h, y], do_ss.at[h, d - 1], do_rs.at[h, d - 1], y_peer(d)) for d in (1, 3, 2)
-        ])
-        for copy in do_copies[h]:
+    def send_cotangents(d):
+        part = lax.rem(x + d, 4)
+        d_attn = dot(og[part], ow[...], 1, 1).astype(bf16)
+        for h in range(HEADS):
+            dog[y, part, h] = d_attn[:, h * HD : (h + 1) * HD]
+        for e in (1, 3, 2):
+            copy = remote(dog.at[y, part], dog.at[y, part], do_ss.at[d, e - 1], do_rs.at[d, e - 1], y_peer(e))
             copy.start()
-
-    for h in range(HEADS):
-        forward_keys(1, h)
-        weigh(h)
-
-    st_copies = []
-    for h in range(HEADS):
-        for copy in do_copies[h]:
-            copy.wait_recv()
-        deltas(h)
-        st_copies.append([
-            remote(st.at[h, y], st.at[h, y], st_ss.at[h, d - 1], st_rs.at[h, d - 1], y_peer(d)) for d in (1, 3, 2)
-        ])
-        for copy in st_copies[h]:
-            copy.start()
-
-    factors, delta_rows, o_copies = [], [], []
-    for h in range(HEADS):
-        for copy in st_copies[h]:
-            copy.wait_recv()
-        factor, delta = combine(h)
-        factors.append(as_row(factor))
-        delta_rows.append(as_row(delta))
-        for j in range(NQ):
-            o_send[h, j] = (o_t[h, :, pl.ds(j * ROWS, ROWS)] * factor[j : j + 1]).T.astype(bf16)
-        o_copies.append([
+            do_copies.append(copy)
+
+    def cotangents(j, h):
+        return dog[j, :, h].reshape(ROWS, HD)
+
+    def send_o(h):
+        copies = [
             remote(o_send.at[h, lax.rem(y + d, 4)], o_recv.at[h, d - 1], o_ss.at[h, d - 1], o_rs.at[h, d - 1], y_peer(d))
             for d in (1, 3, 2)
-        ])
-        for copy in o_copies[h]:
+        ]
+        for copy in copies:
             copy.start()
+        return copies
 
     sg_copies, zg_copies, dq_copies = {}, {}, []
 
-    def backward(h):
-        factor, delta = factors[h], delta_rows[h]
+    def to_sibling(n, h):
+        sg_copies[n, h] = remote(sib_send.at[n, h], sib_recv.at[n, h], sg_ss.at[n, h], sg_rs.at[n, h], sibling)
+        sg_copies[n, h].start()
+
+    def relay(n, h):
+        sg_copies[n, h].wait_recv()
+        for step in (1, 3, 2, 0):
+            slot = slot_of(0, step)
+            total = part_kv[n, h, slot] + sib_recv[n, h, slot].astype(f32)
+            if step == 0:
+                part_kv[n, h, slot] = total
+            else:
+                z_send[n, h, step - 1] = total.astype(bf16)
+                copy = remote(
+                    z_send.at[n, h, step - 1], z_recv.at[n, h, step - 1], zg_ss.at[n, h, step - 1],
+                    zg_rs.at[n, h, step - 1], z_peer(step),
+                )
+                copy.start()
+                zg_copies[n, h, step] = copy
+
+    def value_part(h):
+        cots = dog[:, :, h].reshape(QN, HD)
+        for first in (4, 6, 0, 2):
+            rows = pl.ds(first * ROWS, 2 * ROWS)
+            probs = (wts[h, rows, :].astype(f32) * factors[h]).astype(bf16)
+            wts[h, rows, :] = probs
+            dv = dot(probs, cots, 1, 0).reshape(2, ROWS, HD)
+            if first >= 4:
+                sib_send[0, h, pl.ds(first - 4, 2)] = dv.astype(bf16)
+            else:
+                part_kv[0, h, pl.ds(first, 2)] = dv
+            if first == 6:
+                to_sibling(0, h)
+
+    def backward(h, then=()):
+        await_all(d_copies[h])
+        delta = as_row(sum(dl[h, g, pl.ds(0, NQ), :] for g in range(4)))
         queries = qg[h].reshape(QN, HD)
-        cots = dog[h].reshape(QN, HD)
+        cots = dog[:, :, h].reshape(QN, HD)
         dq = jnp.zeros((HD, QN), f32)
         for t, first in enumerate((4, 6, 0, 2)):
             rows = pl.ds(first * ROWS, 2 * ROWS)
             keys = kg[h, pl.ds(first, 2)].reshape(2 * ROWS, HD)
             values = vg[h, pl.ds(first, 2)].reshape(2 * ROWS, HD)
             dots = dot(values, cots, 1, 1)
-            probs = wts[h, rows, :].astype(f32) * factor
-            grads = (probs * (dots - delta)).astype(bf16)
-            dv = dot(probs.astype(bf16), cots, 1, 0)
-            dk = dot(grads, queries, 1, 0) * SCALE
+            grads = (wts[h, rows, :].astype(f32) * (dots - delta)).astype(bf16)
+            dk = (dot(grads, queries, 1, 0) * SCALE).reshape(2, ROWS, HD)
             dq = dq + dot(keys, grads, 0, 0)
             if first >= 4:
-                for i in range(2):
-                    sib_send[h, first - 4 + i, 0] = dk[i * ROWS : (i + 1) * ROWS].astype(bf16)
-                    sib_send[h, first - 4 + i, 1] = dv[i * ROWS : (i + 1) * ROWS].astype(bf16)
-                part = pl.ds(first - 4, 2)
-                sg_copies[h, t] = remote(
-                    sib_send.at[h, part], sib_recv.at[h, part], sg_ss.at[h, t], sg_rs.at[h, t], sibling
-                )
-                sg_copies[h, t].start()
+                sib_send[1, h, pl.ds(first - 4, 2)] = dk.astype(bf16)
             else:
-                sg_copies[h, t - 2].wait_recv()
-                for i in range(2):
-                    slot = first + i
-                    step = (slot + 1) % 4
-                    for n, grad in enumerate((dk, dv)):
-                        both = grad[i * ROWS : (i + 1) * ROWS] + sib_recv[h, slot, n].astype(f32)
-                        if step == 0:
-                            own_kv[h, n] = both
-                        else:
-                            z_send[h, step - 1, n] = both.astype(bf16)
-                    if step != 0:
-                        zg_copies[h, step] = remote(
-                            z_send.at[h, step - 1], z_recv.at[h, step - 1], zg_ss.at[h, step - 1], zg_rs.at[h, step - 1],
-                            z_peer(step),
-                        )
-                        zg_copies[h, step].start()
+                part_kv[1, h, pl.ds(first, 2)] = dk
+            if first == 6:
+                to_sibling(1, h)
+            if t < len(then) and then[t] is not None:
+                then[t]()
         for j in range(NQ):
             dq_send[h, j] = (dq[:, j * ROWS : (j + 1) * ROWS] * SCALE).T.astype(bf16)
         dq_copies.append([
@@ -282,6 +280,51 @@
         for copy in dq_copies[h]:
             copy.start()
 
+    st_copies, do_copies, d_copies, o_copies, factors = [], [], [], [], []
+    for copy in local:
+        copy.wait()
+    send_cotangents(0)
+    for copy in x_copies[:2]:
+        copy.wait_recv()
+    send_cotangents(1)
+    send_cotangents(3)
+    forward(0, 0)
+    await_forwarded(0, 0)
+    await_all(q_copies[0])
+    scores(0)
+    st_copies.append(share(st, st_ss, st_rs, 0))
+    forward(0, 1)
+
+    x_copies[2].wait_recv()
+    send_cotangents(2)
+
+    for h in (1, 2):
+        await_forwarded(0, h)
+        await_all(q_copies[h])
+        if h == 1:
+            forward(0, 2)
+        else:
+            forward(1, 0)
+        scores(h)
+        st_copies.append(share(st, st_ss, st_rs, h))
+
+    for h in range(HEADS):
+        if h < 2:
+            forward(1, h + 1)
+        await_forwarded(1, h)
+        weigh(h)
+        await_all(st_copies[h])
+        factor = combine(h)
+        factors.append(as_row(factor))
+        if h == 0:
+            await_all(do_copies)
+        deltas(h, factor)
+        d_copies.append(share(dl, d_ss, d_rs, h))
+        value_part(h)
+        o_copies.append(send_o(h))
+        if h > 0:
+            relay(0, h - 1)
+
     def finish(h):
         for copy in dq_copies[h]:
             copy.wait_recv()
@@ -289,32 +332,32 @@
         for i in range(3):
             dq = dq + dq_recv[h, i].astype(f32)
         dq_out[:, cols(h)] = dq.astype(bf16)
-        for step in (1, 2, 3):
-            zg_copies[h, step].wait_recv()
-        for n, out in enumerate((dk_out, dv_out)):
-            total = own_kv[h, n]
-            for i in range(3):
-                total = total + z_recv[h, i, n].astype(f32)
+        for n, out in enumerate((dv_out, dk_out)):
+            total = part_kv[n, h, slot_of(0, 0)]
+            for step in (1, 2, 3):
+                zg_copies[n, h, step].wait_recv()
+                total = total + z_recv[n, h, step - 1].astype(f32)
             out[:, cols(h)] = total.astype(bf16)
 
-    backward(0)
-    backward(1)
-
-    for h in range(HEADS):
-        for copy in o_copies[h]:
-            copy.wait_recv()
-        total = o_send[h, y].astype(f32)
-        for i in range(3):
-            total = total + o_recv[h, i].astype(f32)
-        attn[:, cols(h)] = total.astype(bf16)
-    m_send[...] = dot(attn[...], ow[...], 1, 0).astype(bf16).reshape(m_send.shape)
     m_copies = [
         remote(m_send.at[lax.rem(x + d, 4)], m_recv.at[d - 1], m_ss.at[d - 1], m_rs.at[d - 1], x_peer(d)) for d in (1, 3, 2)
     ]
-    for copy in m_copies:
-        copy.start()
-
-    backward(2)
+
+    def project():
+        for h in range(HEADS):
+            await_all(o_copies[h])
+            total = o_send[h, y].astype(f32)
+            for i in range(3):
+                total = total + o_recv[h, i].astype(f32)
+            attn[:, cols(h)] = total.astype(bf16)
+        m_send[...] = dot(attn[...], ow[...], 1, 0).astype(bf16).reshape(m_send.shape)
+        for copy in m_copies:
+            copy.start()
+
+    backward(0, [lambda: relay(0, 2)])
+    backward(1, [lambda: relay(1, 0), project])
+    backward(2, [lambda: relay(1, 1)])
+    relay(1, 2)
     finish(0)
     finish(1)
     for copy in m_copies:
@@ -327,11 +370,16 @@
 
     for copy in x_copies + m_copies:
         copy.wait_send()
-    for group in q_copies + do_copies + st_copies + o_copies + dq_copies + list(kv_copies.values()) + list(fw_copies.values()):
+    for group in q_copies + [do_copies] + st_copies + d_copies + o_copies + dq_copies + list(kv_copies.values()) + list(fw_copies.values()):
         for copy in group:
             copy.wait_send()
     for copy in list(sg_copies.values()) + list(zg_copies.values()):
         copy.wait_send()
+
+
+def hand_over(*refs):
+    for src, dst in zip(refs[:4], refs[4:]):
+        dst[...] = src[...]
 
 
 def on_device(
@@ -349,7 +397,7 @@
 
     scratch = [
         pltpu.VMEM((HEADS, NQ, ROWS, HD), bf16),
-        pltpu.VMEM((HEADS, NQ, ROWS, HD), bf16),
+        pltpu.VMEM((NQ, 4, HEADS, part, HD), bf16),
         pltpu.VMEM((HEADS, NK, ROWS, HD), bf16),
         pltpu.VMEM((HEADS, NK, ROWS, HD), bf16),
         pltpu.VMEM((HEADS, KN, QN), bf16),
@@ -359,17 +407,18 @@
         pltpu.VMEM((HEADS * HD, width), bf16),
         pltpu.VMEM((4, part, width), bf16),
         pltpu.VMEM((HEADS, HD, QN), f32),
-        pltpu.VMEM((HEADS, 4, 16, ROWS), f32),
+        pltpu.VMEM((HEADS, 4, 8, ROWS), f32),
+        pltpu.VMEM((HEADS, 4, 8, ROWS), f32),
         pltpu.VMEM(own, bf16),
         pltpu.VMEM((HEADS, NQ, ROWS, HD), bf16),
         pltpu.VMEM((HEADS, 3, ROWS, HD), bf16),
         pltpu.VMEM((HEADS, NQ, ROWS, HD), bf16),
         pltpu.VMEM((HEADS, 3, ROWS, HD), bf16),
-        pltpu.VMEM((HEADS, 4, 2, ROWS, HD), bf16),
-        pltpu.VMEM((HEADS, 4, 2, ROWS, HD), bf16),
-        pltpu.VMEM((HEADS, 3, 2, ROWS, HD), bf16),
-        pltpu.VMEM((HEADS, 3, 2, ROWS, HD), bf16),
-        pltpu.VMEM((HEADS, 2, ROWS, HD), f32),
+        pltpu.VMEM((2, HEADS, 4, ROWS, HD), bf16),
+        pltpu.VMEM((2, HEADS, 4, ROWS, HD), bf16),
+        pltpu.VMEM((2, HEADS, 3, ROWS, HD), bf16),
+        pltpu.VMEM((2, HEADS, 3, ROWS, HD), bf16),
+        pltpu.VMEM((2, HEADS, 4, ROWS, HD), f32),
         pltpu.VMEM((4, part, width), bf16),
         pltpu.VMEM((3, part, width), bf16),
         sem(11),
@@ -377,17 +426,18 @@
         sem(2, HEADS, 3), sem(2, HEADS, 3),
         sem(2, HEADS, 4), sem(2, HEADS, 4),
         sem(3), sem(3),
+        sem(4, 3), sem(4, 3),
         sem(HEADS, 3), sem(HEADS, 3),
         sem(HEADS, 3), sem(HEADS, 3),
         sem(HEADS, 3), sem(HEADS, 3),
         sem(HEADS, 3), sem(HEADS, 3),
-        sem(HEADS, 2), sem(HEADS, 2),
-        sem(HEADS, 3), sem(HEADS, 3),
+        sem(2, HEADS), sem(2, HEADS),
+        sem(2, HEADS, 3), sem(2, HEADS, 3),
         sem(3), sem(3),
     ]
-    return pl.pallas_call(
+    results = pl.pallas_call(
         kernel,
-        out_shape=[jax.ShapeDtypeStruct((part, width), bf16)] + [jax.ShapeDtypeStruct(own, bf16)] * 3,
+        out_shape=[pltpu.VMEM((part, width), bf16)] + [pltpu.VMEM(own, bf16)] * 3,
         in_specs=[hbm] * 5 + [smem, vmem, smem],
         out_specs=[vmem] * 4,
         scratch_shapes=scratch,
@@ -399,6 +449,13 @@
         query_states, key_states, value_states, out_weight, out_grad,
         placement, sink_ids.reshape(1, -1), span_mask,
     )
+    return pl.pallas_call(
+        hand_over,
+        out_shape=[jax.ShapeDtypeStruct(r.shape, r.dtype) for r in results],
+        in_specs=[vmem] * 4,
+        out_specs=[vmem] * 4,
+        name="hand_over",
+    )(*[pltpu.with_memory_space_constraint(r, pltpu.VMEM) for r in results])
 
 
 def solution(mesh):

time: 75 us -> 58.4 us (0.78)
  Pallas kernels: 68.3 us -> 56.9 us
  local copies, waits for them, and re-layouts: 5.58 us -> 0 us
    pallas_call x1 -> x2, Pallas kernels: 68.3 us -> 56.9 us  [the longest x1 56 us: on_device(): pl.pallas_call(kernel, out_shape=[pltpu.VMEM((part, width), bf16)] + [plt...]
    unnamed x6 -> x0, local copies, waits for them, and re-layouts: 5.58 us -> none
where the time goes in v2:
time: 58.4 us; the launch traced here: 57.6 us
  Pallas kernels  56.9 us (97%)
  between operations  0.64 us (1%)
    pallas_call x1, Pallas kernels, on_device(): pl.pallas_call(kernel, out_shape=[pltpu.VMEM((part, width), bf16)] + [plt...  56 us

profile of v2, /device:TPU:0, one launch (start us, length us, event | category | flops | bytes accessed | tf_op | source)
XLA Modules:
  0.0 57.6 jit_solution(14158627676741985865)
XLA Ops:
  0.6 56.0 %attention.1 = (bf16[64,1536]{1,0:T(8,128)(2,1)S(1)}, bf16[256,384]{1,0:T(8,128)(2,1)S(1)}, bf16[256,384]{1,0:T(8,128)(2,1)S(1)}, bf16[256,384]{1,0:T(8,128)(2,1)S(1)}) custom-call(bf16[256,384]{1,0:T(8,128)(2,1)} %q_in.1, bf16[256,384]{1,0:T(8,128)(2,1)} %k_in.1, bf16[256,384]{1,0:T(8,128)(2,1)} %v_in.1, bf16[384,1536]{1,0:T(8,128)(2,1)} %w_in.1, ...), custom_call_target="tpu_custom_call" | custom-call | tf_op jit(solution)/shard_map/attention/pallas_call | solution.py:438
  56.7 0.9 %hand_over.1 = (bf16[64,1536]{1,0:T(8,128)(2,1)}, bf16[256,384]{1,0:T(8,128)(2,1)}, bf16[256,384]{1,0:T(8,128)(2,1)}, bf16[256,384]{1,0:T(8,128)(2,1)}) custom-call(bf16[64,1536]{1,0:T(8,128)(2,1)S(1)} %get-tuple-element.8.refs_0_, bf16[256,384]{1,0:T(8,128)(2,1)S(1)} %get-tuple-element.9.refs_1_, bf16[256,384]{1,0:T(8,128)(2,1)S(1)} %get-tuple-element.10.refs_2_, ...), custom_call_target="tpu_custom_call" | custom-call | tf_op jit(solution)/shard_map/hand_over/pallas_call | solution.py:452

commit v3 on v2

--- a/solution.py
+++ b/solution.py
@@ -32,11 +32,12 @@
 def kernel(
     q_in, k_in, v_in, w_in, g_in, place, sinks, table,
     mixed_out, dq_out, dk_out, dv_out,
-    qg, dog, kg, vg, wts, s_buf, kaug, qaug, ow, og, o_t, st, dl, attn,
+    qg, dog, cot, kg, vg, wts, s_buf, kaug, qaug, ow, og, o_t, st, dl, attn,
     o_send, o_recv, dq_send, dq_recv, sib_send, sib_recv, z_send, z_recv, part_kv, m_send, m_recv,
     local_sem, q_ss, q_rs, kv_ss, kv_rs, fw_ss, fw_rs, x_ss, x_rs, do_ss, do_rs, st_ss, st_rs,
     d_ss, d_rs, o_ss, o_rs, dq_ss, dq_rs, sg_ss, sg_rs, zg_ss, zg_rs, m_ss, m_rs,
 ):
+    part = g_in.shape[0]
     s = lax.axis_index("seq")
     x = lax.axis_index("head")
     c = lax.rem(s, 2)
@@ -74,27 +75,29 @@
     barrier = pltpu.get_barrier_semaphore()
     for peer in peers:
         pl.semaphore_signal(barrier, inc=1, device_id=peer, device_id_type=MESH)
+    for copy in local:
+        copy.wait()
     pl.semaphore_wait(barrier, len(peers))
 
-    x_copies = [remote(g_in, og.at[x], x_ss.at[d - 1], x_rs.at[d - 1], x_peer(d)) for d in (1, 3, 2)]
+    x_copies = [remote(og.at[x], og.at[x], x_ss.at[d - 1], x_rs.at[d - 1], x_peer(d)) for d in (1, 3, 2)]
     q_copies, kv_copies, fw_copies = [], {}, {}
     for copy in x_copies:
         copy.start()
     for h in range(HEADS):
         q_copies.append([
-            remote(q_in.at[:, cols(h)], qg.at[h, y], q_ss.at[h, d - 1], q_rs.at[h, d - 1], y_peer(d)) for d in (1, 3, 2)
+            remote(qg.at[h, y], qg.at[h, y], q_ss.at[h, d - 1], q_rs.at[h, d - 1], y_peer(d)) for d in (1, 3, 2)
         ])
-    for n, (src, dst) in enumerate(((k_in, kg), (v_in, vg))):
+    for n, dst in enumerate((kg, vg)):
         for h in range(HEADS):
             kv_copies[n, h] = [
                 remote(
-                    src.at[:, cols(h)], dst.at[h, slot_of(0, 4 - d)], kv_ss.at[n, h, d - 1], kv_rs.at[n, h, d - 1], z_peer(d)
+                    dst.at[h, slot_of(0, 0)], dst.at[h, slot_of(0, 4 - d)], kv_ss.at[n, h, d - 1], kv_rs.at[n, h, d - 1], z_peer(d)
                 )
                 for d in (1, 3, 2)
             ]
             fw_copies[n, h] = [
                 remote(
-                    src.at[:, cols(h)] if d == 0 else dst.at[h, slot_of(0, 4 - d)],
+                    dst.at[h, slot_of(0, (4 - d) % 4)],
                     dst.at[h, slot_of(1, (4 - d) % 4)],
                     fw_ss.at[n, h, d], fw_rs.at[n, h, d], sibling,
                 )
@@ -186,23 +189,30 @@
         for j in range(NQ):
             part = o_t[h, :, pl.ds(j * ROWS, ROWS)] * factor[j : j + 1]
             o_send[h, j] = part.T.astype(bf16)
-            dl[h, y, pl.ds(j, 1), :] = jnp.sum(part * cotangents(j, h).astype(f32).T, axis=0, keepdims=True)
+            dl[h, y, pl.ds(j, 1), :] = jnp.sum(part * cot[h, pl.ds(j * ROWS, ROWS)].astype(f32).T, axis=0, keepdims=True)
 
     def as_row(a):
         return jnp.concatenate([a[j : j + 1] for j in range(NQ)], axis=1)
 
-    def send_cotangents(d):
-        part = lax.rem(x + d, 4)
-        d_attn = dot(og[part], ow[...], 1, 1).astype(bf16)
+    def send_cotangents(n):
+        groups = (3, 0, 1) if n == 0 else (2,)
+        grad = jnp.concatenate([og[lax.rem(x + d, 4)] for d in groups], axis=0)
+        here = pl.ds(0, 3 * part) if n == 0 else pl.ds(3 * part, part)
+        d_attn = dot(grad, ow[...], 1, 1).astype(bf16)
         for h in range(HEADS):
-            dog[y, part, h] = d_attn[:, h * HD : (h + 1) * HD]
-        for e in (1, 3, 2):
-            copy = remote(dog.at[y, part], dog.at[y, part], do_ss.at[d, e - 1], do_rs.at[d, e - 1], y_peer(e))
-            copy.start()
-            do_copies.append(copy)
-
-    def cotangents(j, h):
-        return dog[j, :, h].reshape(ROWS, HD)
+            dog[h, y, here] = d_attn[:, h * HD : (h + 1) * HD]
+            for e in (1, 3, 2):
+                copy = remote(
+                    dog.at[h, y, here], dog.at[h, y, here], do_ss.at[n, h, e - 1], do_rs.at[n, h, e - 1], y_peer(e)
+                )
+                copy.start()
+                do_copies[h].append(copy)
+
+    def order_cotangents(h):
+        for j in range(NQ):
+            for i in range(4):
+                first = pl.multiple_of(lax.rem(i + 5 - x, 4) * part, part)
+                cot[h, pl.ds(j * ROWS + i * part, part)] = dog[h, j, pl.ds(first, part)]
 
     def send_o(h):
         copies = [
@@ -236,7 +246,7 @@
                 zg_copies[n, h, step] = copy
 
     def value_part(h):
-        cots = dog[:, :, h].reshape(QN, HD)
+        cots = cot[h]
         for first in (4, 6, 0, 2):
             rows = pl.ds(first * ROWS, 2 * ROWS)
             probs = (wts[h, rows, :].astype(f32) * factors[h]).astype(bf16)
@@ -246,14 +256,12 @@
                 sib_send[0, h, pl.ds(first - 4, 2)] = dv.astype(bf16)
             else:
                 part_kv[0, h, pl.ds(first, 2)] = dv
-            if first == 6:
-                to_sibling(0, h)
 
     def backward(h, then=()):
         await_all(d_copies[h])
         delta = as_row(sum(dl[h, g, pl.ds(0, NQ), :] for g in range(4)))
         queries = qg[h].reshape(QN, HD)
-        cots = dog[:, :, h].reshape(QN, HD)
+        cots = cot[h]
         dq = jnp.zeros((HD, QN), f32)
         for t, first in enumerate((4, 6, 0, 2)):
             rows = pl.ds(first * ROWS, 2 * ROWS)
@@ -267,10 +275,8 @@
                 sib_send[1, h, pl.ds(first - 4, 2)] = dk.astype(bf16)
             else:
                 part_kv[1, h, pl.ds(first, 2)] = dk
-            if first == 6:
+            if first == 6 and h == HEADS - 1:
                 to_sibling(1, h)
-            if t < len(then) and then[t] is not None:
-                then[t]()
         for j in range(NQ):
             dq_send[h, j] = (dq[:, j * ROWS : (j + 1) * ROWS] * SCALE).T.astype(bf16)
         dq_copies.append([
@@ -279,15 +285,15 @@
         ])
         for copy in dq_copies[h]:
             copy.start()
-
-    st_copies, do_copies, d_copies, o_copies, factors = [], [], [], [], []
-    for copy in local:
-        copy.wait()
-    send_cotangents(0)
+        if h < HEADS - 1:
+            to_sibling(1, h)
+        for step in then:
+            step()
+
+    st_copies, do_copies, d_copies, o_copies, factors = [], [[], [], []], [], [], []
     for copy in x_copies[:2]:
         copy.wait_recv()
-    send_cotangents(1)
-    send_cotangents(3)
+    send_cotangents(0)
     forward(0, 0)
     await_forwarded(0, 0)
     await_all(q_copies[0])
@@ -296,7 +302,7 @@
     forward(0, 1)
 
     x_copies[2].wait_recv()
-    send_cotangents(2)
+    send_cotangents(1)
 
     for h in (1, 2):
         await_forwarded(0, h)
@@ -312,15 +318,16 @@
         if h < 2:
             forward(1, h + 1)
         await_forwarded(1, h)
+        await_all(st_copies[h])
+        await_all(do_copies[h])
         weigh(h)
-        await_all(st_copies[h])
         factor = combine(h)
         factors.append(as_row(factor))
-        if h == 0:
-            await_all(do_copies)
+        order_cotangents(h)
         deltas(h, factor)
+        value_part(h)
         d_copies.append(share(dl, d_ss, d_rs, h))
-        value_part(h)
+        to_sibling(0, h)
         o_copies.append(send_o(h))
         if h > 0:
             relay(0, h - 1)
@@ -370,7 +377,7 @@
 
     for copy in x_copies + m_copies:
         copy.wait_send()
-    for group in q_copies + [do_copies] + st_copies + d_copies + o_copies + dq_copies + list(kv_copies.values()) + list(fw_copies.values()):
+    for group in q_copies + do_copies + st_copies + d_copies + o_copies + dq_copies + list(kv_copies.values()) + list(fw_copies.values()):
         for copy in group:
             copy.wait_send()
     for copy in list(sg_copies.values()) + list(zg_copies.values()):
@@ -397,7 +404,8 @@
 
     scratch = [
         pltpu.VMEM((HEADS, NQ, ROWS, HD), bf16),
-        pltpu.VMEM((NQ, 4, HEADS, part, HD), bf16),
+        pltpu.VMEM((HEADS, NQ, ROWS, HD), bf16),
+        pltpu.VMEM((HEADS, QN, HD), bf16),
         pltpu.VMEM((HEADS, NK, ROWS, HD), bf16),
         pltpu.VMEM((HEADS, NK, ROWS, HD), bf16),
         pltpu.VMEM((HEADS, KN, QN), bf16),
@@ -426,7 +434,7 @@
         sem(2, HEADS, 3), sem(2, HEADS, 3),
         sem(2, HEADS, 4), sem(2, HEADS, 4),
         sem(3), sem(3),
-        sem(4, 3), sem(4, 3),
+        sem(2, HEADS, 3), sem(2, HEADS, 3),
         sem(HEADS, 3), sem(HEADS, 3),
         sem(HEADS, 3), sem(HEADS, 3),
         sem(HEADS, 3), sem(HEADS, 3),

time: 58.4 us -> 57.6 us (0.986); the launches traced: 57.6 us -> 57.4 us
  no operation moved by 1% of the time
where the time goes in v3:
time: 57.6 us; the launch traced here: 57.4 us
  Pallas kernels  56.8 us (99%)
  between operations  0.64 us (1%)
    pallas_call x1, Pallas kernels, on_device(): pl.pallas_call(kernel, out_shape=[pltpu.VMEM((part, width), bf16)] + [plt...  55.9 us

profile of v3, /device:TPU:0, one launch (start us, length us, event | category | flops | bytes accessed | tf_op | source)
XLA Modules:
  0.0 57.4 jit_solution(4362393621217208819)
XLA Ops:
  0.6 55.9 %attention.1 = (bf16[64,1536]{1,0:T(8,128)(2,1)S(1)}, bf16[256,384]{1,0:T(8,128)(2,1)S(1)}, bf16[256,384]{1,0:T(8,128)(2,1)S(1)}, bf16[256,384]{1,0:T(8,128)(2,1)S(1)}) custom-call(bf16[256,384]{1,0:T(8,128)(2,1)} %q_in.1, bf16[256,384]{1,0:T(8,128)(2,1)} %k_in.1, bf16[256,384]{1,0:T(8,128)(2,1)} %v_in.1, bf16[384,1536]{1,0:T(8,128)(2,1)} %w_in.1, ...), custom_call_target="tpu_custom_call" | custom-call | tf_op jit(solution)/shard_map/attention/pallas_call | solution.py:446
  56.5 0.9 %hand_over.1 = (bf16[64,1536]{1,0:T(8,128)(2,1)}, bf16[256,384]{1,0:T(8,128)(2,1)}, bf16[256,384]{1,0:T(8,128)(2,1)}, bf16[256,384]{1,0:T(8,128)(2,1)}) custom-call(bf16[64,1536]{1,0:T(8,128)(2,1)S(1)} %get-tuple-element.8.refs_0_, bf16[256,384]{1,0:T(8,128)(2,1)S(1)} %get-tuple-element.9.refs_1_, bf16[256,384]{1,0:T(8,128)(2,1)S(1)} %get-tuple-element.10.refs_2_, ...), custom_call_target="tpu_custom_call" | custom-call | tf_op jit(solution)/shard_map/hand_over/pallas_call | solution.py:460

commit v4 on v3

--- a/solution.py
+++ b/solution.py
@@ -277,6 +277,7 @@
                 part_kv[1, h, pl.ds(first, 2)] = dk
             if first == 6 and h == HEADS - 1:
                 to_sibling(1, h)
+                relay(1, h - 1)
         for j in range(NQ):
             dq_send[h, j] = (dq[:, j * ROWS : (j + 1) * ROWS] * SCALE).T.astype(bf16)
         dq_copies.append([
@@ -363,7 +364,7 @@
 
     backward(0, [lambda: relay(0, 2)])
     backward(1, [lambda: relay(1, 0), project])
-    backward(2, [lambda: relay(1, 1)])
+    backward(2)
     relay(1, 2)
     finish(0)
     finish(1)

time: 57.6 us -> 57.2 us (level)
  Pallas kernels: 56.8 us -> 55.9 us
    pallas_call x1, Pallas kernels: 55.9 us -> 55 us  [on_device(): pl.pallas_call(kernel, out_shape=[pltpu.VMEM((part, width), bf16)] + [plt...]
where the time goes in v4:
time: 57.2 us; the launch traced here: 56.6 us
  Pallas kernels  55.9 us (98%)
  between operations  0.64 us (1%)
    pallas_call x1, Pallas kernels, on_device(): pl.pallas_call(kernel, out_shape=[pltpu.VMEM((part, width), bf16)] + [plt...  55 us

profile of v4, /device:TPU:0, one launch (start us, length us, event | category | flops | bytes accessed | tf_op | source)
XLA Modules:
  0.0 56.6 jit_solution(691029194875781259)
XLA Ops:
  0.6 55.0 %attention.1 = (bf16[64,1536]{1,0:T(8,128)(2,1)S(1)}, bf16[256,384]{1,0:T(8,128)(2,1)S(1)}, bf16[256,384]{1,0:T(8,128)(2,1)S(1)}, bf16[256,384]{1,0:T(8,128)(2,1)S(1)}) custom-call(bf16[256,384]{1,0:T(8,128)(2,1)} %q_in.1, bf16[256,384]{1,0:T(8,128)(2,1)} %k_in.1, bf16[256,384]{1,0:T(8,128)(2,1)} %v_in.1, bf16[384,1536]{1,0:T(8,128)(2,1)} %w_in.1, ...), custom_call_target="tpu_custom_call" | custom-call | tf_op jit(solution)/shard_map/attention/pallas_call | solution.py:447
  55.6 0.9 %hand_over.1 = (bf16[64,1536]{1,0:T(8,128)(2,1)}, bf16[256,384]{1,0:T(8,128)(2,1)}, bf16[256,384]{1,0:T(8,128)(2,1)}, bf16[256,384]{1,0:T(8,128)(2,1)}) custom-call(bf16[64,1536]{1,0:T(8,128)(2,1)S(1)} %get-tuple-element.8.refs_0_, bf16[256,384]{1,0:T(8,128)(2,1)S(1)} %get-tuple-element.9.refs_1_, bf16[256,384]{1,0:T(8,128)(2,1)S(1)} %get-tuple-element.10.refs_2_, ...), custom_call_target="tpu_custom_call" | custom-call | tf_op jit(solution)/shard_map/hand_over/pallas_call | solution.py:461
